TPU v7x, 256 devices: a whole 4x4x8 slice. The times are simulated.
256 devices in a mesh: seq: 64 (over z, y, core), grp: 4 (over x).
Axes of the slice: x: 4, y: 4, z: 8, core: 2. Of those that a mesh axis runs over, the one named last changes fastest.
Arguments:
- queries: bfloat16 [4, 8192, 8192], P('grp', 'seq'), may hold values from -6 to 6
- keys_values: bfloat16 [2, 64, 128, 8192], P(None, 'seq', 'grp'), may hold values from -6 to 6
- neighbours: int32 [4, 128, 2], P('grp'), may hold values from 0 to 63, all different within a row
- grad_context: bfloat16 [4, 8192, 8192], P('grp', 'seq'), may hold values from -6 to 6
Outputs:
- context: bfloat16 [4, 8192, 8192], P('grp', 'seq')
- d_queries: bfloat16 [4, 8192, 8192], P('grp', 'seq')
- d_keys_values: bfloat16 [2, 64, 128, 8192], P(None, 'seq', 'grp')
Inputs may be any that keep to these rules, and one draw needn't show every extreme that they name: `neighbours`: the 2 blocks of one span differ, and every block is retrieved by some span.
All inputs are finite; a program needn't handle non-finite values.
Results may differ from a plain program's by a relative error of at most 0.015.
Values may be sent and summed in bfloat16 or wider, within the bound.
A program may use at most 128 MiB of HBM per device.

v0:
```python
import math

import jax
import jax.numpy as jnp
from jax import lax
from jax.sharding import PartitionSpec as P

SPAN = 64
NBR = 2


def sequence_pass(query_seq, keyval_head, cotangent_seq, span_links):
    length = query_seq.shape[0]
    head_dim = query_seq.shape[1]
    margin = SPAN - 1
    blocks_all = keyval_head.shape[1]
    rows_block = keyval_head.shape[2]
    num_spans = length // SPAN
    per_step = min(num_spans, max(1, 2048 // SPAN))
    step_count = num_spans // per_step
    scaling = 1.0 / math.sqrt(head_dim)
    pad_rows = jnp.zeros((margin, head_dim), jnp.bfloat16)
    shifted_query = jnp.concatenate([query_seq[margin:], pad_rows], 0).reshape(
        step_count, per_step, SPAN, head_dim
    )
    shifted_grad = jnp.concatenate([cotangent_seq[margin:], pad_rows], 0).reshape(
        step_count, per_step, SPAN, head_dim
    )
    links = span_links.reshape(step_count, per_step, NBR)

    def one_step(grad_blocks, pieces):
        query_block, grad_block, link_block = pieces
        key_rows = keyval_head[0][link_block].reshape(per_step, NBR * rows_block, head_dim)
        value_rows = keyval_head[1][link_block].reshape(per_step, NBR * rows_block, head_dim)
        scores = (
            jnp.einsum("cqd,ckd->cqk", query_block, key_rows, preferred_element_type=jnp.float32)
            * scaling
        )
        largest = jnp.max(scores, axis=-1, keepdims=True)
        exponent = jnp.exp(scores - largest)
        weights = exponent / jnp.sum(exponent, axis=-1, keepdims=True)
        weights_low = weights.astype(jnp.bfloat16)
        attended = jnp.einsum(
            "cqk,ckd->cqd", weights_low, value_rows, preferred_element_type=jnp.float32
        ).astype(jnp.bfloat16)
        grad_weights = jnp.einsum(
            "cqd,ckd->cqk", grad_block, value_rows, preferred_element_type=jnp.float32
        )
        row_total = jnp.sum(grad_weights * weights, axis=-1, keepdims=True)
        grad_scores = (weights * (grad_weights - row_total) * scaling).astype(jnp.bfloat16)
        grad_query = jnp.einsum(
            "cqk,ckd->cqd", grad_scores, key_rows, preferred_element_type=jnp.float32
        ).astype(jnp.bfloat16)
        grad_keys = jnp.einsum(
            "cqk,cqd->ckd", grad_scores, query_block, preferred_element_type=jnp.float32
        )
        grad_values = jnp.einsum(
            "cqk,cqd->ckd", weights_low, grad_block, preferred_element_type=jnp.float32
        )
        stacked = jnp.stack(
            [
                grad_keys.reshape(per_step, NBR, rows_block, head_dim),
                grad_values.reshape(per_step, NBR, rows_block, head_dim),
            ],
            2,
        )
        stacked = stacked.reshape(per_step * NBR, 2, rows_block, head_dim)
        flat_links = link_block.reshape(-1)
        grad_blocks = grad_blocks + jax.ops.segment_sum(
            stacked, flat_links, num_segments=blocks_all
        )
        return (grad_blocks, (attended, grad_query))

    start_grad = jnp.zeros((blocks_all, 2, rows_block, head_dim), jnp.float32)
    grad_blocks, (attended, grad_query) = lax.scan(
        one_step, start_grad, (shifted_query, shifted_grad, links)
    )
    grad_blocks = jnp.transpose(grad_blocks, (1, 0, 2, 3))
    attended = attended.reshape(length, head_dim)
    grad_query = grad_query.reshape(length, head_dim)
    context = jnp.concatenate([pad_rows, attended[: length - margin]], 0)
    query_back = jnp.concatenate([pad_rows, grad_query[: length - margin]], 0)
    return (context, query_back, grad_blocks)


def per_device(queries, keys_values, neighbours, grad_context):
    query_seq, cotangent_seq = (
        lax.all_to_all(queries, "seq", split_axis=2, concat_axis=1, tiled=True),
        lax.all_to_all(grad_context, "seq", split_axis=2, concat_axis=1, tiled=True),
    )
    whole_rows = lax.all_gather(keys_values, "grp", axis=2, tiled=True)
    keyval_head = lax.all_to_all(whole_rows, "seq", split_axis=3, concat_axis=1, tiled=True)
    context, query_back, grad_blocks = sequence_pass(
        query_seq[0], keyval_head, cotangent_seq[0], neighbours[0]
    )
    context_out, d_queries = (
        lax.all_to_all(context[None], "seq", split_axis=1, concat_axis=2, tiled=True),
        lax.all_to_all(query_back[None], "seq", split_axis=1, concat_axis=2, tiled=True),
    )
    summed_grad = lax.psum_scatter(
        grad_blocks.astype(jnp.bfloat16), "grp", scatter_dimension=2, tiled=True
    )
    d_keys_values = lax.all_to_all(summed_grad, "seq", split_axis=1, concat_axis=3, tiled=True)
    return (context_out, d_queries, d_keys_values)


def solution(mesh):
    in_specs = (
        P("grp", "seq", None),
        P(None, "seq", "grp", None),
        P("grp", None, None),
        P("grp", "seq", None),
    )
    out_specs = (P("grp", "seq", None), P("grp", "seq", None), P(None, "seq", "grp", None))
    return jax.shard_map(
        per_device, mesh=mesh, in_specs=in_specs, out_specs=out_specs, check_vma=False
    )
```

profile of v0, /device:TPU:1, one launch (start us, length us, event | category | flops | bytes accessed | tf_op | source)
XLA Modules:
  0.0 923.3 jit_solution(1838280026461039883)
XLA Ops:
  7.2 9.5 %copy.58 = bf16[1,128,8192]{1,0,2:T(2,128)(2,1)} copy(bf16[1,128,8192]{2,1,0:T(8,128)(2,1)} %param.6) | data formatting | bytes 4194304 | tf_op args[0]
  17.2 45.2 %reduce = bf16[8192,128]{1,0:T(8,128)(2,1)S(1)} reduce(bf16[8192,1,128]{2,1,0:T(2,128)(2,1)} %bitcast.139, bf16[]{:T(256)} %broadcast.66), dimensions={1}, to_apply=%bitcast.81.reduce_sub_computation | reduce | bytes 4194306
  64.4 13.3 %all-to-all-start = ((bf16[64,2,8192]{2,1,0:T(2,128)(2,1)}), bf16[64,2,8192]{2,1,0:T(2,128)(2,1)S(1)}, u32[]{:S(2)}, u32[]{:S(2)}) async-start(bf16[64,2,8192]{2,1,0:T(2,128)(2,1)} %reshape.101), calls=%async_computation | async-start | bytes 4194304 | tf_op jit(solution)/shard_map/all_to_all | solution.py:88
  80.0 9.5 %copy.63 = bf16[1,128,8192]{1,0,2:T(2,128)(2,1)} copy(bf16[1,128,8192]{2,1,0:T(8,128)(2,1)} %param.9) | data formatting | bytes 4194304 | tf_op args[3]
  89.5 46.5 %reduce.1 = bf16[8192,128]{1,0:T(8,128)(2,1)} reduce(bf16[8192,1,128]{2,1,0:T(2,128)(2,1)} %bitcast.146, bf16[]{:T(256)} %broadcast.66), dimensions={1}, to_apply=%bitcast.83.reduce_sub_computation | reduce | bytes 4194306
  136.0 4.0 reshape.103
  139.9 10.5 %all-to-all-start.2 = ((bf16[64,2,8192]{2,1,0:T(2,128)(2,1)}), bf16[64,2,8192]{2,1,0:T(2,128)(2,1)}, u32[]{:S(2)}, u32[]{:S(2)}) async-start(bf16[64,2,8192]{2,1,0:T(2,128)(2,1)} %reshape.103), calls=%async_computation.2 | async-start | bytes 4194304 | tf_op jit(solution)/shard_map/all_to_all | solution.py:89
  150.5 14.8 %copy.61 = bf16[2,1,128,8192]{2,0,1,3:T(2,128)(2,1)} copy(bf16[2,1,128,8192]{3,0,1,2:T(2,128)(2,1)} %all-gather.2.cloned.1.call-done) | data formatting | bytes 8388608 | tf_op jit(solution)/shard_map/all_gather | solution.py:91
  165.3 34.8 %all-to-all-done.2 = bf16[64,2,8192]{2,1,0:T(2,128)(2,1)} async-done(((bf16[64,2,8192]{2,1,0:T(2,128)(2,1)}), bf16[64,2,8192]{2,1,0:T(2,128)(2,1)}, u32[]{:S(2)}, u32[]{:S(2)}) %all-to-all-start.2) | async-done | bytes 2097184 | tf_op jit(solution)/shard_map/all_to_all | solution.py:89
  200.0 7.2 all-to-all-start.1
  207.4 6.8 reshape.102
  216.7 3.0 copy.59
  219.6 3.5 slice.26
  223.1 10.5 %reshape.104 = bf16[8192,1,128]{2,1,0:T(2,128)(2,1)} reshape(bf16[64,2,8192]{2,1,0:T(2,128)(2,1)} %all-to-all-done.2) | data formatting | bytes 4194304
  236.0 3.0 copy.64
  244.2 57.6 %all-to-all-done.1 = bf16[2,1,128,8192]{2,0,1,3:T(2,128)(2,1)} async-done(((bf16[2,1,128,8192]{2,0,1,3:T(2,128)(2,1)}), bf16[2,1,128,8192]{2,0,1,3:T(2,128)(2,1)}, u32[]{:S(2)}, u32[]{:S(2)}) %all-to-all-start.1) | async-done | bytes 4194336 | tf_op jit(solution)/shard_map/all_to_all | solution.py:92
  301.9 4.7 copy.62
  306.5 6.4 copy.66
  312.9 4.3 broadcast.41
  317.2 315.3 %while.14 = (s32[]{:T(128)}, f32[64,2,128,128]{3,2,1,0:T(8,128)}, bf16[4,32,64,128]{3,2,1,0:T(8,128)(2,1)}, bf16[4,32,64,128]{3,2,1,0:T(8,128)(2,1)}, s32[4,32,2...) while((s32[]{:T(128)}, f32[64,2,128,128]{3,2,1,0:T(8,128)}, ...), condition=%wide.region_5.6_spmd, body=%wide.region_0.5_spmd.sunk | while | flops 821041088 | bytes 129073328 | solution.py:75
  318.0 4.0 slice_bitcast_fusion.3
  326.7 3.2 fusion.93
  329.9 4.1 fusion.91
  334.0 16.1 %fusion.96 = bf16[4,32,64,128]{3,2,1,0:T(8,128)(2,1)} fusion(bf16[4,32,64,128]{3,2,1,0:T(8,128)(2,1)} %get-tuple-element.180, s32[]{:T(128)S(6)} %copy.94, bf16[32,256,128]{2,1,0:T(8,128)(2,1)} %bitcast.136, f32[32,64,256]{2,1,0:T(8,128)} %fusion.93, f32[32,64,256]{2,1,0:T(8,128)} %get-tuple-element.165, f32[32,64]{1,0:T(8,128)S(1)} %get-tuple-element.166), kind=kOutput, calls=%fused_computation.21.clone.1 | convolution fusion | flops 138152192 | bytes 11042820 | tf_op jit(solution)/shard_map/while/body/eval_jaxpr/cqk,ckd->cqd/dot_general | solution.py:51
  350.0 2.9 fusion.95
  352.9 17.9 %fusion.94 = f32[32,256,128]{2,1,0:T(8,128)} fusion(f32[32,64,256]{2,1,0:T(8,128)} %fusion.93, bf16[4,32,64,128]{3,2,1,0:T(8,128)(2,1)} %get-tuple-element.191, s32[]{:T(128)S(6)} %copy.94, f32[32,64,256]{2,1,0:T(8,128)} %get-tuple-element.165, f32[32,64]{1,0:T(8,128)S(1)} %get-tuple-element.166), kind=kOutput, calls=%fused_computation.15.clone.1 | convolution fusion | flops 137890048 | bytes 13139972 | tf_op jit(solution)/shard_map/while/body/eval_jaxpr/cqk,cqd->ckd/dot_general | solution.py:54
  373.2 3.8 pad_maximum_fusion.2
  377.0 19.1 %scatter_fusion = f32[64,2,128,128]{3,2,1,0:T(8,128)} fusion(f32[64,2,128,128]{3,2,1,0:T(8,128)} %get-tuple-element.178, s32[64]{0:T(128)S(1)} %reshape.123, f32[64,2,128,128]{3,2,1,0:T(8,128)} %pad_maximum_fusion.2), kind=kCustom, calls=%fused_computation.2.clone.1 | custom fusion | flops 2097152 | bytes 25166080 | tf_op jit(solution)/shard_map/while/body/eval_jaxpr/scatter-add | solution.py:69
  396.5 4.0 slice_bitcast_fusion.3
  405.2 3.2 fusion.93
  408.4 4.1 fusion.91
  412.5 16.1 %fusion.96 = bf16[4,32,64,128]{3,2,1,0:T(8,128)(2,1)} fusion(bf16[4,32,64,128]{3,2,1,0:T(8,128)(2,1)} %get-tuple-element.180, s32[]{:T(128)S(6)} %copy.94, bf16[32,256,128]{2,1,0:T(8,128)(2,1)} %bitcast.136, f32[32,64,256]{2,1,0:T(8,128)} %fusion.93, f32[32,64,256]{2,1,0:T(8,128)} %get-tuple-element.165, f32[32,64]{1,0:T(8,128)S(1)} %get-tuple-element.166), kind=kOutput, calls=%fused_computation.21.clone.1 | convolution fusion | flops 138152192 | bytes 11042820 | tf_op jit(solution)/shard_map/while/body/eval_jaxpr/cqk,ckd->cqd/dot_general | solution.py:51
  428.6 2.9 fusion.95
  431.5 17.9 %fusion.94 = f32[32,256,128]{2,1,0:T(8,128)} fusion(f32[32,64,256]{2,1,0:T(8,128)} %fusion.93, bf16[4,32,64,128]{3,2,1,0:T(8,128)(2,1)} %get-tuple-element.191, s32[]{:T(128)S(6)} %copy.94, f32[32,64,256]{2,1,0:T(8,128)} %get-tuple-element.165, f32[32,64]{1,0:T(8,128)S(1)} %get-tuple-element.166), kind=kOutput, calls=%fused_computation.15.clone.1 | convolution fusion | flops 137890048 | bytes 13139972 | tf_op jit(solution)/shard_map/while/body/eval_jaxpr/cqk,cqd->ckd/dot_general | solution.py:54
  451.7 3.8 pad_maximum_fusion.2
  455.5 19.3 %scatter_fusion = f32[64,2,128,128]{3,2,1,0:T(8,128)} fusion(f32[64,2,128,128]{3,2,1,0:T(8,128)} %get-tuple-element.178, s32[64]{0:T(128)S(1)} %reshape.123, f32[64,2,128,128]{3,2,1,0:T(8,128)} %pad_maximum_fusion.2), kind=kCustom, calls=%fused_computation.2.clone.1 | custom fusion | flops 2097152 | bytes 25166080 | tf_op jit(solution)/shard_map/while/body/eval_jaxpr/scatter-add | solution.py:69
  475.2 4.0 slice_bitcast_fusion.3
  483.9 3.2 fusion.93
  487.1 4.1 fusion.91
  491.2 16.1 %fusion.96 = bf16[4,32,64,128]{3,2,1,0:T(8,128)(2,1)} fusion(bf16[4,32,64,128]{3,2,1,0:T(8,128)(2,1)} %get-tuple-element.180, s32[]{:T(128)S(6)} %copy.94, bf16[32,256,128]{2,1,0:T(8,128)(2,1)} %bitcast.136, f32[32,64,256]{2,1,0:T(8,128)} %fusion.93, f32[32,64,256]{2,1,0:T(8,128)} %get-tuple-element.165, f32[32,64]{1,0:T(8,128)S(1)} %get-tuple-element.166), kind=kOutput, calls=%fused_computation.21.clone.1 | convolution fusion | flops 138152192 | bytes 11042820 | tf_op jit(solution)/shard_map/while/body/eval_jaxpr/cqk,ckd->cqd/dot_general | solution.py:51
  510.2 17.9 %fusion.94 = f32[32,256,128]{2,1,0:T(8,128)} fusion(f32[32,64,256]{2,1,0:T(8,128)} %fusion.93, bf16[4,32,64,128]{3,2,1,0:T(8,128)(2,1)} %get-tuple-element.191, s32[]{:T(128)S(6)} %copy.94, f32[32,64,256]{2,1,0:T(8,128)} %get-tuple-element.165, f32[32,64]{1,0:T(8,128)S(1)} %get-tuple-element.166), kind=kOutput, calls=%fused_computation.15.clone.1 | convolution fusion | flops 137890048 | bytes 13139972 | tf_op jit(solution)/shard_map/while/body/eval_jaxpr/cqk,cqd->ckd/dot_general | solution.py:54
  530.5 3.8 pad_maximum_fusion.2
  534.3 19.3 %scatter_fusion = f32[64,2,128,128]{3,2,1,0:T(8,128)} fusion(f32[64,2,128,128]{3,2,1,0:T(8,128)} %get-tuple-element.178, s32[64]{0:T(128)S(1)} %reshape.123, f32[64,2,128,128]{3,2,1,0:T(8,128)} %pad_maximum_fusion.2), kind=kCustom, calls=%fused_computation.2.clone.1 | custom fusion | flops 2097152 | bytes 25166080 | tf_op jit(solution)/shard_map/while/body/eval_jaxpr/scatter-add | solution.py:69
  554.0 4.0 slice_bitcast_fusion.3
  562.7 3.2 fusion.93
  565.9 4.1 fusion.91
  570.0 16.1 %fusion.96 = bf16[4,32,64,128]{3,2,1,0:T(8,128)(2,1)} fusion(bf16[4,32,64,128]{3,2,1,0:T(8,128)(2,1)} %get-tuple-element.180, s32[]{:T(128)S(6)} %copy.94, bf16[32,256,128]{2,1,0:T(8,128)(2,1)} %bitcast.136, f32[32,64,256]{2,1,0:T(8,128)} %fusion.93, f32[32,64,256]{2,1,0:T(8,128)} %get-tuple-element.165, f32[32,64]{1,0:T(8,128)S(1)} %get-tuple-element.166), kind=kOutput, calls=%fused_computation.21.clone.1 | convolution fusion | flops 138152192 | bytes 11042820 | tf_op jit(solution)/shard_map/while/body/eval_jaxpr/cqk,ckd->cqd/dot_general | solution.py:51
  589.0 17.9 %fusion.94 = f32[32,256,128]{2,1,0:T(8,128)} fusion(f32[32,64,256]{2,1,0:T(8,128)} %fusion.93, bf16[4,32,64,128]{3,2,1,0:T(8,128)(2,1)} %get-tuple-element.191, s32[]{:T(128)S(6)} %copy.94, f32[32,64,256]{2,1,0:T(8,128)} %get-tuple-element.165, f32[32,64]{1,0:T(8,128)S(1)} %get-tuple-element.166), kind=kOutput, calls=%fused_computation.15.clone.1 | convolution fusion | flops 137890048 | bytes 13139972 | tf_op jit(solution)/shard_map/while/body/eval_jaxpr/cqk,cqd->ckd/dot_general | solution.py:54
  609.2 3.8 pad_maximum_fusion.2
  613.0 19.3 %scatter_fusion = f32[64,2,128,128]{3,2,1,0:T(8,128)} fusion(f32[64,2,128,128]{3,2,1,0:T(8,128)} %get-tuple-element.178, s32[64]{0:T(128)S(1)} %reshape.123, f32[64,2,128,128]{3,2,1,0:T(8,128)} %pad_maximum_fusion.2), kind=kCustom, calls=%fused_computation.2.clone.1 | custom fusion | flops 2097152 | bytes 25166080 | tf_op jit(solution)/shard_map/while/body/eval_jaxpr/scatter-add | solution.py:69
  634.2 6.3 convert_bitcast_fusion
  641.1 33.3 %copy.82 = bf16[1,8192,128]{2,0,1:T(2,128)(2,1)} copy(bf16[1,8192,128]{2,1,0:T(8,128)(2,1)S(1)} %pad_bitcast_fusion.1) | data formatting | bytes 4194304 | tf_op jit(solution)/shard_map/broadcast_in_dim | solution.py:97
  674.3 45.2 %reduce.2 = bf16[8192,128]{1,0:T(8,128)(2,1)S(1)} reduce(bf16[8192,1,128]{2,1,0:T(2,128)(2,1)} %bitcast.143, bf16[]{:T(256)} %broadcast.66), dimensions={1}, to_apply=%bitcast.98.reduce_sub_computation | reduce | bytes 4194306
  721.5 7.0 all-to-all-start.3
  730.8 33.3 %copy.81 = bf16[1,8192,128]{2,0,1:T(2,128)(2,1)} copy(bf16[1,8192,128]{2,1,0:T(8,128)(2,1)S(1)} %pad_bitcast_fusion) | data formatting | bytes 4194304 | tf_op jit(solution)/shard_map/broadcast_in_dim | solution.py:98
  764.1 46.5 %reduce.3 = bf16[8192,128]{1,0:T(8,128)(2,1)} reduce(bf16[8192,1,128]{2,1,0:T(2,128)(2,1)} %bitcast.140, bf16[]{:T(256)} %broadcast.66), dimensions={1}, to_apply=%bitcast.97.reduce_sub_computation | reduce | bytes 4194306
  810.6 4.0 reshape.107
  814.6 60.1 %all_to_all.102 = bf16[64,2,8192]{2,1,0:T(2,128)(2,1)} all-to-all(bf16[64,2,8192]{2,1,0:T(2,128)(2,1)} %reshape.107), channel_id=1, replica_groups=mesh['seq'=64,'grp'=4] {'seq'}, dimensions={0} | all-to-all | bytes 4194304 | tf_op jit(solution)/shard_map/all_to_all | solution.py:98
  874.7 7.0 all-to-all-start.5
  881.7 6.8 reshape.106
  893.8 4.2 copy.72
  898.0 6.8 reshape.108
  907.3 2.9 copy.70
  910.2 4.1 copy.73
  (96 shorter events, 67.2 us)
Async XLA Ops:
  64.4 13.5 %copy-start.4 = (bf16[2,1,32,8192]{3,2,1,0:T(8,128)(2,1)S(1)}, bf16[2,1,32,8192]{3,2,1,0:T(8,128)(2,1)}, u32[]{:S(2)}) copy-start(bf16[2,1,32,8192]{3,2,1,0:T(8,128)(2,1)} %param.7) | copy-start | bytes 3145732
  64.4 75.6 %all-to-all-start = ((bf16[64,2,8192]{2,1,0:T(2,128)(2,1)}), bf16[64,2,8192]{2,1,0:T(2,128)(2,1)S(1)}, u32[]{:S(2)}, u32[]{:S(2)}) async-start(bf16[64,2,8192]{2,1,0:T(2,128)(2,1)} %reshape.101), calls=%async_computation | async-start | bytes 4194304 | tf_op jit(solution)/shard_map/all_to_all | solution.py:88
  77.7 72.8 %all-gather.2.cloned.1.call-start = ((), (), s32[]{:S(2)}) async-start(), calls=%async_computation.7 | async-start | bytes 5242880 | tf_op jit(solution)/shard_map/all_gather | solution.py:91
  139.9 60.1 %all-to-all-start.2 = ((bf16[64,2,8192]{2,1,0:T(2,128)(2,1)}), bf16[64,2,8192]{2,1,0:T(2,128)(2,1)}, u32[]{:S(2)}, u32[]{:S(2)}) async-start(bf16[64,2,8192]{2,1,0:T(2,128)(2,1)} %reshape.103), calls=%async_computation.2 | async-start | bytes 4194304 | tf_op jit(solution)/shard_map/all_to_all | solution.py:89
  165.3 42.1 %copy-start.5 = (s32[1,128,2]{1,2,0:T(2,128)S(1)}, s32[1,128,2]{1,2,0:T(2,128)}, u32[]{:S(2)}) copy-start(s32[1,128,2]{1,2,0:T(2,128)} %param.8) | copy-start | bytes 3076
  200.0 101.8 %all-to-all-start.1 = ((bf16[2,1,128,8192]{2,0,1,3:T(2,128)(2,1)}), bf16[2,1,128,8192]{2,0,1,3:T(2,128)(2,1)}, u32[]{:S(2)}, u32[]{:S(2)}) async-start(bf16[2,1,128,8192]{2,0,1,3:T(2,128)(2,1)} %copy.61), calls=%async_computation.1 | async-start | bytes 8388608 | tf_op jit(solution)/shard_map/all_to_all | solution.py:92
  207.3 667.4 %reduce-scatter.2.cloned.1.call-start = ((), (), s32[]{:S(2)}) async-start(), calls=%async_computation.8 | async-start | bytes 5242880 | tf_op jit(solution)/shard_map/reduce_scatter | solution.py:100
  239.0 2.3 copy-start.3
  352.9 17.9 %copy-start.1 = (f32[32,64,256]{2,1,0:T(8,128)S(1)}, f32[32,64,256]{2,1,0:T(8,128)}, u32[]{:S(2)}) copy-start(f32[32,64,256]{2,1,0:T(8,128)} %get-tuple-element.165) | copy-start | bytes 6291460 | tf_op jit(solution)/shard_map/while
  370.8 2.4 copy-start
  431.5 17.9 %copy-start.1 = (f32[32,64,256]{2,1,0:T(8,128)S(1)}, f32[32,64,256]{2,1,0:T(8,128)}, u32[]{:S(2)}) copy-start(f32[32,64,256]{2,1,0:T(8,128)} %get-tuple-element.165) | copy-start | bytes 6291460 | tf_op jit(solution)/shard_map/while
  449.3 2.4 copy-start
  510.2 17.9 %copy-start.1 = (f32[32,64,256]{2,1,0:T(8,128)S(1)}, f32[32,64,256]{2,1,0:T(8,128)}, u32[]{:S(2)}) copy-start(f32[32,64,256]{2,1,0:T(8,128)} %get-tuple-element.165) | copy-start | bytes 6291460 | tf_op jit(solution)/shard_map/while
  528.1 2.4 copy-start
  589.0 17.9 %copy-start.1 = (f32[32,64,256]{2,1,0:T(8,128)S(1)}, f32[32,64,256]{2,1,0:T(8,128)}, u32[]{:S(2)}) copy-start(f32[32,64,256]{2,1,0:T(8,128)} %get-tuple-element.165) | copy-start | bytes 6291460 | tf_op jit(solution)/shard_map/while
  606.8 2.4 copy-start
  721.5 93.1 %all-to-all-start.3 = ((bf16[64,2,8192]{2,1,0:T(2,128)(2,1)}), bf16[64,2,8192]{2,1,0:T(2,128)(2,1)S(1)}, u32[]{:S(2)}, u32[]{:S(2)}) async-start(bf16[64,2,8192]{2,1,0:T(2,128)(2,1)} %reshape.105), calls=%async_computation.3 | async-start | bytes 4194304 | tf_op jit(solution)/shard_map/all_to_all | solution.py:97
  874.7 39.6 %all-to-all-start.5 = ((bf16[2,64,32,128]{3,2,0,1:T(8,128)(2,1)}), bf16[2,64,32,128]{3,2,0,1:T(8,128)(2,1)S(1)}, u32[]{:S(2)}, u32[]{:S(2)}) async-start(bf16[2,64,32,128]{3,2,0,1:T(8,128)(2,1)} %reduce-scatter.2.cloned.1.call-done), calls=%async_computation.6 | async-start | bytes 2097152 | tf_op jit(solution)/shard_map/all_to_all | solution.py:103
  893.8 4.2 copy-start.2
Sparse Core Ops, SparseCore 0:
  80.9 51.7 all-gather.1
  640.6 47.7 reduce-scatter.1
where the time goes:
time: 932 us; the launch traced here: 923 us
  other arithmetic  282 us (30%)
  local copies, waits for them, and re-layouts  242 us (26%)
  matrix products  186 us (20%)
  waiting for transfers between devices  92.5 us (10%)
  blocking collectives  60.1 us (6%)
  starting transfers between devices  45.3 us (5%)
  between operations  14.5 us (2%)
    unnamed x4, other arithmetic  183 us
    unnamed x26, local copies, waits for them, and re-layouts  82.5 us
    scatter-add x4, other arithmetic, one_step(): jax.ops.segment_sum(stacked, flat_links, num_segments=blocks_all)  76.9 us
    dot_general x4, matrix products, one_step(): jnp.einsum('cqk,cqd->ckd', grad_scores, query_block, preferred_element_ty...  71.5 us
    dot_general x4, matrix products, one_step(): jnp.einsum('cqk,ckd->cqd', grad_scores, key_rows, preferred_element_type=...  64.2 us
    all_to_all x1, blocking collectives, per_device(): lax.all_to_all(query_back[None], 'seq', split_axis=1, concat_axis=2, tile...  60.1 us
    all_to_all x1, waiting for transfers between devices, per_device(): lax.all_to_all(whole_rows, 'seq', split_axis=3, concat_axis=1, tiled=True)  57.6 us
    all_to_all x1, waiting for transfers between devices, per_device(): lax.all_to_all(grad_context, 'seq', split_axis=2, concat_axis=1, tiled=True)  34.8 us
  transfers between devices with their start and end apart: 7, of which 2 were waited for; matrix products, arithmetic and copies ran while one was open for 34% of the time, Pallas kernels for 0%

commit v1 on v0

v1 whole, which is shorter than its diff:
```python
import functools
import math

import jax
import jax.numpy as jnp
from jax import lax
from jax.experimental import pallas as pl
from jax.experimental.pallas import tpu as pltpu
from jax.sharding import PartitionSpec as P

SPAN = 64
NBR = 2
HEAD = 128
PLANE = 8
MESH = pl.DeviceIdType.MESH
BF16 = jnp.bfloat16
F32 = jnp.float32


def dot_nt(a, b):
    return lax.dot_general(a, b, (((1,), (1,)), ((), ())), preferred_element_type=F32)


def dot_nn(a, b):
    return lax.dot_general(a, b, (((1,), (0,)), ((), ())), preferred_element_type=F32)


def dot_tn(a, b):
    return lax.dot_general(a, b, (((0,), (0,)), ((), ())), preferred_element_type=F32)


def kernel(nz, nx, meta, q_in, kv_in, g_in, ctx_out, dq_out, dkv_out,
           kv_a, kv_b, q_a, q_b, g_a, g_b, ctx_a, ctx_b, dq_a, dq_b,
           sum_k, sum_v, part_a, part_b, half_a, half_b, full_a, full_b,
           own_a, own_b, roll_c, roll_d,
           in_send, in_recv, ag_send, ag_recv, rs_send, rs_recv, out_send, out_recv):
    np_ = nx * PLANE
    tokens = q_in.shape[1]
    rows = kv_in.shape[2]
    spans = PLANE * tokens // SPAN + 1
    slots = spans * nx * NBR
    far = nz // 2
    scaling = 1.0 / math.sqrt(HEAD)
    seq = lax.axis_index("seq")
    x = lax.axis_index("grp")
    z = seq // PLANE
    yc = seq % PLANE
    me = x * PLANE + yc
    kv = (kv_a, kv_b)
    q = (q_a, q_b)
    g = (g_a, g_b)
    ctx = (ctx_a, ctx_b)
    dq = (dq_a, dq_b)
    part = (part_a, part_b)
    half = (half_a, half_b)
    full = (full_a, full_b)
    own = (own_a, own_b)

    def zone(zz):
        return pl.ds(pl.multiple_of(zz * PLANE, PLANE), PLANE)

    def near(offset):
        return (z + offset + nz) % nz

    def z_device(offset):
        return (near(offset) * PLANE + yc, x)

    def peer(r):
        m = (me + r) % np_
        return m, m // PLANE, m % PLANE

    def columns(m, h):
        return pl.ds(pl.multiple_of((m * 2 + h) * HEAD, HEAD), HEAD)

    zero_rows = jnp.zeros((nx, SPAN, HEAD), BF16)
    for h in range(2):
        for buf in (q[h], g[h]):
            buf[:, :16, :] = jnp.zeros((nx, 16, HEAD), BF16)
            buf[:, 16 + PLANE * tokens:, :] = zero_rows
    sum_k[0] = jnp.zeros((HEAD, HEAD), F32)
    sum_v[0] = jnp.zeros((HEAD, HEAD), F32)

    barrier = pltpu.get_barrier_semaphore()

    def greet(r, carry):
        m, px, pyc = peer(r)
        pl.semaphore_signal(barrier, inc=1, device_id=(z * PLANE + pyc, px), device_id_type=MESH)
        return carry

    lax.fori_loop(1, np_, greet, 0)
    for offset in (-1, 1):
        pl.semaphore_signal(barrier, inc=1, device_id=z_device(offset), device_id_type=MESH)
    pl.semaphore_wait(barrier, np_ + 1)

    def tok_rows(k):
        return pl.ds(pl.multiple_of(16 + k * tokens, 16), tokens)

    def blk_rows(k):
        return pl.ds(pl.multiple_of(k * rows, rows), rows)

    def kv_dst(h):
        return kv[h].at[:, seq, blk_rows(x), :]

    def q_dst(buf):
        return buf.at[x, tok_rows(yc), :]

    def send_kv(h):
        def body(r, carry):
            m, px, pyc = peer(r)
            pltpu.make_async_remote_copy(
                src_ref=kv_in.at[:, 0, :, columns(m, h)], dst_ref=kv_dst(h),
                send_sem=in_send.at[h], recv_sem=in_recv.at[h],
                device_id=(z * PLANE + pyc, px), device_id_type=MESH).start()
            return carry
        pltpu.make_async_copy(kv_in.at[:, 0, :, columns(me, h)], kv_dst(h), in_recv.at[h]).start()
        lax.fori_loop(1, np_, body, 0)

    def send_qg(h):
        def body(r, carry):
            m, px, pyc = peer(r)
            for k, (src, dst) in enumerate(((q_in, q[h]), (g_in, g[h]))):
                sem = 2 + 2 * k + h
                pltpu.make_async_remote_copy(
                    src_ref=src.at[0, :, columns(m, h)], dst_ref=q_dst(dst),
                    send_sem=in_send.at[sem], recv_sem=in_recv.at[sem],
                    device_id=(z * PLANE + pyc, px), device_id_type=MESH).start()
            return carry
        for k, (src, dst) in enumerate(((q_in, q[h]), (g_in, g[h]))):
            pltpu.make_async_copy(
                src.at[0, :, columns(me, h)], q_dst(dst), in_recv.at[2 + 2 * k + h]).start()
        lax.fori_loop(1, np_, body, 0)

    def wait_bytes(ref, sem):
        pltpu.make_async_copy(ref, ref, sem).wait()

    def wait_kv(h):
        wait_bytes(kv[h].at[:, zone(z)], in_recv.at[h])

    def wait_qg(h):
        for k, buf in enumerate((q[h], g[h])):
            wait_bytes(buf.at[:, pl.ds(16, PLANE * tokens), :], in_recv.at[2 + 2 * k + h])

    def wait_in_sends():
        for h in range(2):
            wait_bytes(kv_in.at[:, 0, :, pl.ds(0, (np_ - 1) * HEAD)], in_send.at[h])
            for k, src in enumerate((q_in, g_in)):
                wait_bytes(src.at[0, :, pl.ds(0, (np_ - 1) * HEAD)], in_send.at[2 + 2 * k + h])

    def ag_copy(h, way, step, kind):
        sign = 1 - 2 * way
        part_ref = kv[h].at[kind, zone(near(-sign * (step - 1)))]
        return pltpu.make_async_remote_copy(
            src_ref=part_ref, dst_ref=part_ref,
            send_sem=ag_send.at[h, way, step - 1, kind], recv_sem=ag_recv.at[h, way, step - 1, kind],
            device_id=z_device(sign), device_id_type=MESH)

    def ag_has(way, step, kind):
        return step < far or kind == way

    def ag_start(h, step, kind):
        for way in range(2):
            if ag_has(way, step, kind):
                ag_copy(h, way, step, kind).start()

    def ag_wait(h, way, step, kind):
        sign = 1 - 2 * way
        wait_bytes(kv[h].at[kind, zone(near(-sign * step))], ag_recv.at[h, way, step - 1, kind])

    def ag_forward(h, step, kind):
        for way in range(2):
            ag_wait(h, way, step - 1, kind)
            if ag_has(way, step, kind):
                ag_copy(h, way, step, kind).start()

    def ag_last(h):
        for kind in range(2):
            for way in range(2):
                if ag_has(way, far, kind):
                    ag_wait(h, way, far, kind)

    def rs_send_step(h, step):
        for way in range(2):
            sign = 1 - 2 * way
            zz = zone(near(sign * (far + 1 - step)))
            if step == 1:
                src, dst = part[h].at[way, zz], half[h].at[way]
            else:
                src, dst = part[h].at[:, zz], full[h].at[way, step - 2]
            pltpu.make_async_remote_copy(
                src_ref=src, dst_ref=dst,
                send_sem=rs_send.at[h, way, step - 1], recv_sem=rs_recv.at[h, way, step - 1],
                device_id=z_device(sign), device_id_type=MESH).start()

    def rs_wait(h, way, step):
        ref = half[h].at[way] if step == 1 else full[h].at[way, step - 2]
        wait_bytes(ref, rs_recv.at[h, way, step - 1])

    def rs_step(h, step):
        for way in range(2):
            sign = 1 - 2 * way
            base = near(sign * (far + 1 - step)) * PLANE
            rs_wait(h, way, step - 1)

            def add(b, carry):
                if step == 2:
                    part[h][way, base + b] = (
                        part[h][way, base + b].astype(F32) + half[h][way, b].astype(F32)).astype(BF16)
                else:
                    for kind in range(2):
                        part[h][kind, base + b] = (
                            part[h][kind, base + b].astype(F32)
                            + full[h][way, step - 3, kind, b].astype(F32)).astype(BF16)
                return carry

            lax.fori_loop(0, PLANE, add, 0)
        rs_send_step(h, step)

    def rs_last(h):
        for way in range(2):
            rs_wait(h, way, far)

        def add(b, carry):
            for kind in range(2):
                total = part[h][kind, z * PLANE + b].astype(F32)
                for way in range(2):
                    if far > 1:
                        total += full[h][way, far - 2, kind, b].astype(F32)
                    elif kind == way:
                        total += half[h][way, b].astype(F32)
                own[h][kind, b] = total.astype(BF16)
            return carry

        lax.fori_loop(0, PLANE, add, 0)

        def body(r, carry):
            m, px, pyc = peer(r)
            pltpu.make_async_remote_copy(
                src_ref=own[h].at[:, pyc, blk_rows(px), :], dst_ref=dkv_out.at[:, 0, :, columns(me, h)],
                send_sem=out_send.at[h], recv_sem=out_recv.at[0],
                device_id=(z * PLANE + pyc, px), device_id_type=MESH).start()
            return carry

        pltpu.make_async_copy(
            own[h].at[:, yc, blk_rows(x), :], dkv_out.at[:, 0, :, columns(me, h)], out_recv.at[0]).start()
        lax.fori_loop(1, np_, body, 0)

    def out_rows(k):
        return pl.ds(pl.multiple_of(SPAN + k * tokens, 16), tokens)

    def send_out(h):
        def body(r, carry):
            m, px, pyc = peer(r)
            for k, (src, dst) in enumerate(((ctx[h], ctx_out), (dq[h], dq_out))):
                pltpu.make_async_remote_copy(
                    src_ref=src.at[px, out_rows(pyc), :], dst_ref=dst.at[0, :, columns(me, h)],
                    send_sem=out_send.at[2 + 2 * k + h], recv_sem=out_recv.at[1 + k],
                    device_id=(z * PLANE + pyc, px), device_id_type=MESH).start()
            return carry
        for k, (src, dst) in enumerate(((ctx[h], ctx_out), (dq[h], dq_out))):
            pltpu.make_async_copy(
                src.at[x, out_rows(yc), :], dst.at[0, :, columns(me, h)], out_recv.at[1 + k]).start()
        lax.fori_loop(1, np_, body, 0)

    def compute(h, events):
        row_id = lax.broadcasted_iota(jnp.int32, (SPAN, HEAD), 0)

        def shifted(buf, s, v):
            wide = buf[s, pl.ds(pl.multiple_of(v * SPAN, SPAN), SPAN + 16), :].astype(F32)
            return pltpu.roll(wide, SPAN + 1, 0)[:SPAN].astype(BF16)

        def store_back(out, hold, s, v, value):
            rolled = pltpu.roll(value, SPAN - 1, 0)
            out[s, pl.ds(pl.multiple_of(v * SPAN, SPAN), SPAN), :] = jnp.where(
                row_id == SPAN - 1, rolled, hold[s]).astype(BF16)
            hold[s] = rolled

        def step(v, carry):
            head_start = jnp.logical_and(z == 0, v == 0)
            keep = jnp.where(head_start, 0.0, 1.0)
            for s in range(nx):
                slot = (v * nx + s) * NBR
                qs = shifted(q[h], s, v)
                gs = (shifted(g[h], s, v).astype(F32) * keep).astype(BF16)
                link = [meta[slot + j] for j in range(NBR)]
                keys = jnp.concatenate([kv[h][0, link[j]] for j in range(NBR)], 0)
                vals = jnp.concatenate([kv[h][1, link[j]] for j in range(NBR)], 0)
                scores = dot_nt(qs, keys)
                grad_w = dot_nt(gs, vals)
                largest = jnp.max(scores, axis=-1, keepdims=True)
                expo = jnp.exp2((scores - largest) * (scaling * math.log2(math.e)))
                weights = expo * (1.0 / jnp.sum(expo, axis=-1, keepdims=True))
                low = weights.astype(BF16)
                total = jnp.sum(grad_w * weights, axis=-1, keepdims=True)
                grad_s = (weights * (grad_w - total) * scaling).astype(BF16)
                store_back(ctx[h], roll_c, s, v, dot_nn(low, vals) * keep)
                store_back(dq[h], roll_d, s, v, dot_nn(grad_s, keys))
                grad_k = dot_tn(grad_s, qs)
                grad_v = dot_tn(low, gs)
                for j in range(NBR):
                    before = meta[slots + slot + j]
                    cut = slice(j * HEAD, (j + 1) * HEAD)
                    sum_k[slot + j + 1] = sum_k[before] + grad_k[cut]
                    sum_v[slot + j + 1] = sum_v[before] + grad_v[cut]
            for when, event in events:
                pl.when(v == min(when, spans - 1))(event)
            return carry

        lax.fori_loop(0, spans, step, 0)

        def gather(b, carry):
            last = meta[2 * slots + b]
            part[h][0, b] = sum_k[last].astype(BF16)
            part[h][1, b] = sum_v[last].astype(BF16)
            return carry

        lax.fori_loop(0, nz * PLANE, gather, 0)

    send_kv(0)
    send_kv(1)
    send_qg(0)
    wait_kv(0)
    for kind in range(2):
        ag_start(0, 1, kind)
    send_qg(1)
    for step in range(2, far + 1):
        for kind in range(2):
            ag_forward(0, step, kind)
    wait_kv(1)
    for kind in range(2):
        ag_start(1, 1, kind)
    ag_last(0)
    wait_qg(0)
    events = []
    at = [4, 7, 11, 14, 16, 16]
    for step in range(2, far + 1):
        for kind in range(2):
            events.append((at[len(events)], functools.partial(ag_forward, 1, step, kind)))
    compute(0, events)
    rs_send_step(0, 1)
    send_out(0)
    ag_last(1)
    wait_qg(1)
    events = []
    at = [3, 8, 14]
    for step in range(2, far + 1):
        events.append((at[len(events)], functools.partial(rs_step, 0, step)))
    compute(1, events)
    rs_send_step(1, 1)
    send_out(1)
    rs_last(0)
    for step in range(2, far + 1):
        rs_step(1, step)
    rs_last(1)

    wait_in_sends()
    for h in range(2):
        for way in range(2):
            for step in range(1, far + 1):
                for kind in range(2):
                    if ag_has(way, step, kind):
                        ag_copy(h, way, step, kind).wait_send()
                ref = half[h].at[way] if step == 1 else full[h].at[way, step - 2]
                wait_bytes(ref, rs_send.at[h, way, step - 1])
        wait_bytes(dkv_out.at[:, 0, :, pl.ds(0, (np_ - 1) * HEAD)], out_send.at[h])
        for k, dst in enumerate((ctx_out, dq_out)):
            wait_bytes(dst.at[0, :, pl.ds(0, (np_ - 1) * HEAD)], out_send.at[2 + 2 * k + h])
    for k, dst in enumerate((dkv_out, ctx_out, dq_out)):
        wait_bytes(dst, out_recv.at[k])


def make_meta(neighbours, nz, nx):
    nblk = nz * PLANE
    z = lax.axis_index("seq") // PLANE
    links = lax.all_gather(neighbours[0], "grp", axis=0, tiled=False)
    per_plane = links.shape[1] // nz
    links = jnp.concatenate([jnp.zeros((nx, 1, NBR), jnp.int32), links], 1)
    links = lax.dynamic_slice_in_dim(links, z * per_plane, per_plane + 1, 1)
    links = jnp.transpose(links, (1, 0, 2)).reshape(-1)
    n = links.shape[0]
    ids = jnp.arange(n, dtype=jnp.int32)
    same = (links[:, None] == links[None, :]) & (ids[None, :] < ids[:, None])
    before = jnp.max(jnp.where(same, ids[None, :] + 1, 0), axis=1)
    here = links[None, :] == jnp.arange(nblk, dtype=jnp.int32)[:, None]
    last = jnp.max(jnp.where(here, ids[None, :] + 1, 0), axis=1)
    return jnp.concatenate([links, before, last])


def solution(mesh):
    nz = mesh.shape["seq"] // PLANE
    nx = mesh.shape["grp"]
    far = nz // 2

    def step(queries, keys_values, neighbours, grad_context):
        meta = make_meta(neighbours, nz, nx)
        tokens = queries.shape[1]
        nblk = nz * PLANE
        long_in = 16 + PLANE * tokens + SPAN
        long_out = PLANE * tokens + SPAN
        slots = (PLANE * tokens // SPAN + 1) * nx * NBR
        sem = pltpu.SemaphoreType.DMA
        twice = lambda shape: [pltpu.VMEM(shape, BF16)] * 2
        scratch = (
            twice((2, nblk, HEAD, HEAD))
            + twice((nx, long_in, HEAD)) + twice((nx, long_in, HEAD))
            + twice((nx, long_out, HEAD)) + twice((nx, long_out, HEAD))
            + [pltpu.VMEM((slots + 1, HEAD, HEAD), F32)] * 2
            + twice((2, nblk, HEAD, HEAD))
            + twice((2, PLANE, HEAD, HEAD))
            + twice((2, max(far - 1, 1), 2, PLANE, HEAD, HEAD))
            + twice((2, PLANE, HEAD, HEAD))
            + [pltpu.VMEM((nx, SPAN, HEAD), F32)] * 2
            + [sem((6,)), sem((6,)), sem((2, 2, far, 2)), sem((2, 2, far, 2)),
               sem((2, 2, far)), sem((2, 2, far)), sem((6,)), sem((3,))]
        )
        hbm = pl.BlockSpec(memory_space=pl.ANY)
        out = pl.pallas_call(
            functools.partial(kernel, nz, nx),
            out_shape=(
                jax.ShapeDtypeStruct(queries.shape, BF16),
                jax.ShapeDtypeStruct(queries.shape, BF16),
                jax.ShapeDtypeStruct(keys_values.shape, BF16),
            ),
            in_specs=[pl.BlockSpec(memory_space=pltpu.SMEM), hbm, hbm, hbm],
            out_specs=(hbm, hbm, hbm),
            scratch_shapes=scratch,
            compiler_params=pltpu.CompilerParams(
                collective_id=0, has_side_effects=True, vmem_limit_bytes=60 * 1024 * 1024
            ),
            name="plane_attention",
        )(meta, queries, keys_values, grad_context)
        return tuple(out)

    in_specs = (
        P("grp", "seq", None),
        P(None, "seq", "grp", None),
        P("grp", None, None),
        P("grp", "seq", None),
    )
    out_specs = (P("grp", "seq", None), P("grp", "seq", None), P(None, "seq", "grp", None))
    return jax.shard_map(step, mesh=mesh, in_specs=in_specs, out_specs=out_specs, check_vma=False)
```

time: 932 us -> 235 us (0.25)
  other arithmetic: 282 us -> 0.97 us
  local copies, waits for them, and re-layouts: 242 us -> 6.52 us
  Pallas kernels: 0 us -> 218 us
  matrix products: 186 us -> 0 us
  waiting for transfers between devices: 92.5 us -> 0 us
  blocking collectives: 60.1 us -> 8.78 us
  starting transfers between devices: 45.3 us -> 0 us
  between operations: 14.5 us -> 0.69 us
    pallas_call x0 -> x1, Pallas kernels: none -> 218 us  [step(): pl.pallas_call(functools.partial(kernel, nz, nx), out_shape=(jax.ShapeDty...]
    unnamed x4 -> x0, other arithmetic: 183 us -> none
    dot_general x20 -> x0, matrix products: 170 us -> none  [the longest x4 71.5 us: one_step(): jnp.einsum('cqk,cqd->ckd', grad_scores, query_block, preferred_element_ty...]
    all_to_all x5 -> x0, waiting for transfers between devices: 92.4 us -> none  [the longest x1 57.6 us: per_device(): lax.all_to_all(whole_rows, 'seq', split_axis=3, concat_axis=1, tiled=True)]
    scatter-add x4 -> x0, other arithmetic: 76.9 us -> none  [one_step(): jax.ops.segment_sum(stacked, flat_links, num_segments=blocks_all)]
    unnamed x26 -> x7, local copies, waits for them, and re-layouts: 82.5 us -> 6.18 us
    broadcast_in_dim x4 -> x0, local copies, waits for them, and re-layouts: 67.7 us -> none  [the longest x2 33.8 us: per_device(): context[None]]
    all_to_all x1 -> x0, blocking collectives: 60.1 us -> none  [per_device(): lax.all_to_all(query_back[None], 'seq', split_axis=1, concat_axis=2, tile...]
  transfers between devices with their start and end apart: 7 -> 0, of which waited for: 2 -> 0; matrix products, arithmetic and copies ran while one was open for 34% -> 0% of each run, Pallas kernels for 0% -> 0%
where the time goes in v1:
time: 235 us
  Pallas kernels  218 us (93%)
  blocking collectives  8.78 us (4%)
  local copies, waits for them, and re-layouts  6.52 us (3%)
    pallas_call x1, Pallas kernels, step(): pl.pallas_call(functools.partial(kernel, nz, nx), out_shape=(jax.ShapeDty...  218 us
    all_gather x1, blocking collectives, make_meta(): links = lax.all_gather(neighbours[0], 'grp', axis=0, tiled=False)  8.78 us
    unnamed x7, local copies, waits for them, and re-layouts  6.18 us

profile of v1, /device:TPU:1, one launch (start us, length us, event | category | flops | bytes accessed | tf_op | source)
XLA Modules:
  0.0 234.7 jit_solution(1585709538517234453)
XLA Ops:
  0.7 8.8 %all_gather.3 = s32[4,128,2]{1,2,0:T(2,128)S(1)} all-gather(s32[1,128,2]{1,2,0:T(2,128)} %param.6), channel_id=1, replica_groups=mesh['seq'=64,'grp'=4] {'grp'}, dimensions={0}, use_global_device_ids=true | all-gather | bytes 5120 | tf_op jit(solution)/shard_map/all_gather | solution.py:374
  9.4 0.1 fusion.1
  9.5 0.1 copy.9
  9.6 0.1 reshape.16
  9.8 0.1 select_reduce_fusion.1
  9.9 0.2 select_reduce_fusion
  10.1 0.7 pad_add_fusion.meta
  10.8 217.7 %plane_attention.1 = (bf16[1,128,8192]{2,1,0:T(8,128)(2,1)}, bf16[1,128,8192]{2,1,0:T(8,128)(2,1)}, bf16[2,1,32,8192]{3,2,1,0:T(8,128)(2,1)}) custom-call(s32[336]{0:T(512)} %pad_add_fusion.meta, bf16[1,128,8192]{2,1,0:T(8,128)(2,1)} %q_in.1, bf16[2,1,32,8192]{3,2,1,0:T(8,128)(2,1)} %kv_in.1, bf16[1,128,8192]{2,1,0:T(8,128)(2,1)} %g_in.1), custom_call_target="tpu_custom_call" | custom-call | tf_op jit(solution)/shard_map/plane_attention/pallas_call | solution.py:416
  228.5 0.0 copy-start
  228.5 3.2 %copy.13 = bf16[1,128,8192]{2,1,0:T(8,128)(2,1)} copy(bf16[1,128,8192]{2,1,0:T(8,128)(2,1)} %get-tuple-element.6) | data formatting | bytes 4194304
  231.7 0.0 copy-done
  231.7 0.0 copy-start.1
  231.8 1.3 copy.14
  233.1 0.6 copy-done.1
  233.7 1.0 copy.15
  (1 shorter events, 0.0 us)
Async XLA Ops:
  228.5 3.3 %copy-start = (bf16[1,128,8192]{2,1,0:T(8,128)(2,1)S(1)}, bf16[1,128,8192]{2,1,0:T(8,128)(2,1)}, u32[]{:S(2)}) copy-start(bf16[1,128,8192]{2,1,0:T(8,128)(2,1)} %get-tuple-element.7) | copy-start | bytes 6291460
  231.7 2.0 copy-start.1

commit v2 on v1

--- a/solution.py
+++ b/solution.py
@@ -11,6 +11,8 @@
 SPAN = 64
 NBR = 2
 HEAD = 128
+AT_A0, AT_A1 = 6, 12
+AT_B0, AT_B1, AT_B2 = 4, 9, 14
 PLANE = 8
 MESH = pl.DeviceIdType.MESH
 BF16 = jnp.bfloat16
@@ -29,16 +31,15 @@
     return lax.dot_general(a, b, (((0,), (0,)), ((), ())), preferred_element_type=F32)
 
 
-def kernel(nz, nx, meta, q_in, kv_in, g_in, ctx_out, dq_out, dkv_out,
+def kernel(nz, nx, links_in, q_in, kv_in, g_in, ctx_out, dq_out, dkv_out,
            kv_a, kv_b, q_a, q_b, g_a, g_b, ctx_a, ctx_b, dq_a, dq_b,
            sum_k, sum_v, part_a, part_b, half_a, half_b, full_a, full_b,
-           own_a, own_b, roll_c, roll_d,
-           in_send, in_recv, ag_send, ag_recv, rs_send, rs_recv, out_send, out_recv):
+           own_a, own_b, roll_c, roll_d, links, before_v, last_v, links_s, before_s, last_s,
+           link_send, link_recv, in_send, in_recv, ag_send, ag_recv, rs_send, rs_recv, out_send, out_recv):
     np_ = nx * PLANE
     tokens = q_in.shape[1]
     rows = kv_in.shape[2]
     spans = PLANE * tokens // SPAN + 1
-    slots = spans * nx * NBR
     far = nz // 2
     scaling = 1.0 / math.sqrt(HEAD)
     seq = lax.axis_index("seq")
@@ -146,6 +147,51 @@
             for k, src in enumerate((q_in, g_in)):
                 wait_bytes(src.at[0, :, pl.ds(0, (np_ - 1) * HEAD)], in_send.at[2 + 2 * k + h])
 
+    def send_links():
+        def body(r, carry):
+            pltpu.make_async_remote_copy(
+                src_ref=links_in, dst_ref=links.at[x], send_sem=link_send, recv_sem=link_recv.at[0],
+                device_id=(seq, (x + r) % nx), device_id_type=MESH).start()
+            return carry
+        pltpu.make_async_copy(links_in, links.at[x], link_recv.at[0]).start()
+        lax.fori_loop(1, nx, body, 0)
+
+    def chain_links():
+        wait_bytes(links, link_recv.at[0])
+        copy = pltpu.make_async_copy(links, links_s, link_recv.at[1])
+        copy.start()
+        copy.wait()
+        shape = links.shape[1:]
+        row = lax.broadcasted_iota(jnp.int32, shape, 0)
+        lane = lax.broadcasted_iota(jnp.int32, shape, 1)
+        block = row * shape[1] + lane
+        held = [links[s] for s in range(nx)]
+        slot = [(lane * nx + s) * NBR + row + 1 for s in range(nx)]
+
+        def body(v, carry):
+            before, last = list(carry[:nx]), carry[nx]
+            for s in range(nx):
+                for j in range(NBR):
+                    link = links_s[s, j, v]
+                    here = (v * nx + s) * NBR + j + 1
+                    for t in range(nx):
+                        before[t] = jnp.where(
+                            jnp.logical_and(held[t] == link, slot[t] > here), here, before[t])
+                    last = jnp.where(block == link, here, last)
+            return (*before, last)
+
+        zero = jnp.zeros(shape, jnp.int32)
+        found = lax.fori_loop(0, spans, body, (zero,) * (nx + 1))
+        for s in range(nx):
+            before_v[s] = found[s]
+        last_v[...] = found[nx]
+        copies = (pltpu.make_async_copy(before_v, before_s, link_recv.at[1]),
+                  pltpu.make_async_copy(last_v, last_s, link_recv.at[2]))
+        for copy in copies:
+            copy.start()
+        for copy in copies:
+            copy.wait()
+
     def ag_copy(h, way, step, kind):
         sign = 1 - 2 * way
         part_ref = kv[h].at[kind, zone(near(-sign * (step - 1)))]
@@ -157,8 +203,9 @@
     def ag_has(way, step, kind):
         return step < far or kind == way
 
-    def ag_start(h, step, kind):
-        for way in range(2):
+    def ag_start(h, step, turn):
+        for way in range(2):
+            kind = way if turn == 0 else 1 - way
             if ag_has(way, step, kind):
                 ag_copy(h, way, step, kind).start()
 
@@ -166,8 +213,9 @@
         sign = 1 - 2 * way
         wait_bytes(kv[h].at[kind, zone(near(-sign * step))], ag_recv.at[h, way, step - 1, kind])
 
-    def ag_forward(h, step, kind):
-        for way in range(2):
+    def ag_forward(h, step, turn):
+        for way in range(2):
+            kind = way if turn == 0 else 1 - way
             ag_wait(h, way, step - 1, kind)
             if ag_has(way, step, kind):
                 ag_copy(h, way, step, kind).start()
@@ -178,59 +226,63 @@
                 if ag_has(way, far, kind):
                     ag_wait(h, way, far, kind)
 
-    def rs_send_step(h, step):
-        for way in range(2):
-            sign = 1 - 2 * way
-            zz = zone(near(sign * (far + 1 - step)))
-            if step == 1:
-                src, dst = part[h].at[way, zz], half[h].at[way]
-            else:
-                src, dst = part[h].at[:, zz], full[h].at[way, step - 2]
-            pltpu.make_async_remote_copy(
-                src_ref=src, dst_ref=dst,
-                send_sem=rs_send.at[h, way, step - 1], recv_sem=rs_recv.at[h, way, step - 1],
-                device_id=z_device(sign), device_id_type=MESH).start()
-
-    def rs_wait(h, way, step):
-        ref = half[h].at[way] if step == 1 else full[h].at[way, step - 2]
-        wait_bytes(ref, rs_recv.at[h, way, step - 1])
-
-    def rs_step(h, step):
-        for way in range(2):
-            sign = 1 - 2 * way
-            base = near(sign * (far + 1 - step)) * PLANE
-            rs_wait(h, way, step - 1)
+    def rs_has(way, step, kind):
+        return step > 1 or kind == way
+
+    def rs_dst(h, way, step, kind):
+        return half[h].at[way] if step == 1 else full[h].at[way, step - 2, kind]
+
+    def rs_base(way, step):
+        return near((1 - 2 * way) * (far + 1 - step)) * PLANE
+
+    def rs_send_part(h, way, step, kind):
+        pltpu.make_async_remote_copy(
+            src_ref=part[h].at[kind, pl.ds(pl.multiple_of(rs_base(way, step), PLANE), PLANE)],
+            dst_ref=rs_dst(h, way, step, kind),
+            send_sem=rs_send.at[h, way, step - 1, kind], recv_sem=rs_recv.at[h, way, step - 1, kind],
+            device_id=z_device(1 - 2 * way), device_id_type=MESH).start()
+
+    def rs_wait(h, way, step, kind):
+        wait_bytes(rs_dst(h, way, step, kind), rs_recv.at[h, way, step - 1, kind])
+
+    def rs_begin(h):
+        for way in range(2):
+            rs_send_part(h, way, 1, way)
+        for way in range(2):
+            if far > 1:
+                rs_send_part(h, way, 2, 1 - way)
+
+    def rs_step(h, step, turn):
+        for way in range(2):
+            kind = way if turn == 0 else 1 - way
+            if not rs_has(way, step - 1, kind):
+                continue
+            base = rs_base(way, step)
+            rs_wait(h, way, step - 1, kind)
+            got = rs_dst(h, way, step - 1, kind)
 
             def add(b, carry):
-                if step == 2:
-                    part[h][way, base + b] = (
-                        part[h][way, base + b].astype(F32) + half[h][way, b].astype(F32)).astype(BF16)
-                else:
-                    for kind in range(2):
-                        part[h][kind, base + b] = (
-                            part[h][kind, base + b].astype(F32)
-                            + full[h][way, step - 3, kind, b].astype(F32)).astype(BF16)
+                part[h][kind, base + b] = (
+                    part[h][kind, base + b].astype(F32) + got[b].astype(F32)).astype(BF16)
                 return carry
 
             lax.fori_loop(0, PLANE, add, 0)
-        rs_send_step(h, step)
+            rs_send_part(h, way, step, kind)
 
     def rs_last(h):
-        for way in range(2):
-            rs_wait(h, way, far)
-
-        def add(b, carry):
-            for kind in range(2):
+        for kind in range(2):
+            ways = [way for way in range(2) if rs_has(way, far, kind)]
+            for way in ways:
+                rs_wait(h, way, far, kind)
+
+            def add(b, carry):
                 total = part[h][kind, z * PLANE + b].astype(F32)
-                for way in range(2):
-                    if far > 1:
-                        total += full[h][way, far - 2, kind, b].astype(F32)
-                    elif kind == way:
-                        total += half[h][way, b].astype(F32)
+                for way in ways:
+                    total += rs_dst(h, way, far, kind)[b].astype(F32)
                 own[h][kind, b] = total.astype(BF16)
-            return carry
-
-        lax.fori_loop(0, PLANE, add, 0)
+                return carry
+
+            lax.fori_loop(0, PLANE, add, 0)
 
         def body(r, carry):
             m, px, pyc = peer(r)
@@ -266,7 +318,7 @@
 
         def shifted(buf, s, v):
             wide = buf[s, pl.ds(pl.multiple_of(v * SPAN, SPAN), SPAN + 16), :].astype(F32)
-            return pltpu.roll(wide, SPAN + 1, 0)[:SPAN].astype(BF16)
+            return pltpu.roll(wide, SPAN + 1, 0)[:SPAN]
 
         def store_back(out, hold, s, v, value):
             rolled = pltpu.roll(value, SPAN - 1, 0)
@@ -277,30 +329,34 @@
         def step(v, carry):
             head_start = jnp.logical_and(z == 0, v == 0)
             keep = jnp.where(head_start, 0.0, 1.0)
-            for s in range(nx):
-                slot = (v * nx + s) * NBR
-                qs = shifted(q[h], s, v)
-                gs = (shifted(g[h], s, v).astype(F32) * keep).astype(BF16)
-                link = [meta[slot + j] for j in range(NBR)]
-                keys = jnp.concatenate([kv[h][0, link[j]] for j in range(NBR)], 0)
-                vals = jnp.concatenate([kv[h][1, link[j]] for j in range(NBR)], 0)
-                scores = dot_nt(qs, keys)
-                grad_w = dot_nt(gs, vals)
-                largest = jnp.max(scores, axis=-1, keepdims=True)
-                expo = jnp.exp2((scores - largest) * (scaling * math.log2(math.e)))
+            group = range(nx)
+            slot = [(v * nx + s) * NBR for s in group]
+            link = [[links_s[s, j, v] for j in range(NBR)] for s in group]
+            qs = [shifted(q[h], s, v).astype(BF16) for s in group]
+            gs = [(shifted(g[h], s, v) * keep).astype(BF16) for s in group]
+            keys = [jnp.concatenate([kv[h][0, link[s][j]] for j in range(NBR)], 0) for s in group]
+            vals = [jnp.concatenate([kv[h][1, link[s][j]] for j in range(NBR)], 0) for s in group]
+            scores = [dot_nt(qs[s], keys[s]) for s in group]
+            grad_w = [dot_nt(gs[s], vals[s]) for s in group]
+            low, grad_s = [], []
+            for s in group:
+                largest = jnp.max(scores[s], axis=-1, keepdims=True)
+                expo = jnp.exp2((scores[s] - largest) * (scaling * math.log2(math.e)))
                 weights = expo * (1.0 / jnp.sum(expo, axis=-1, keepdims=True))
-                low = weights.astype(BF16)
-                total = jnp.sum(grad_w * weights, axis=-1, keepdims=True)
-                grad_s = (weights * (grad_w - total) * scaling).astype(BF16)
-                store_back(ctx[h], roll_c, s, v, dot_nn(low, vals) * keep)
-                store_back(dq[h], roll_d, s, v, dot_nn(grad_s, keys))
-                grad_k = dot_tn(grad_s, qs)
-                grad_v = dot_tn(low, gs)
+                low.append(weights.astype(BF16))
+                total = jnp.sum(grad_w[s] * weights, axis=-1, keepdims=True)
+                grad_s.append((weights * (grad_w[s] - total) * scaling).astype(BF16))
+            for s in group:
+                store_back(ctx[h], roll_c, s, v, dot_nn(low[s], vals[s]) * keep)
+                store_back(dq[h], roll_d, s, v, dot_nn(grad_s[s], keys[s]))
+            grad_k = [dot_tn(grad_s[s], qs[s]) for s in group]
+            grad_v = [dot_tn(low[s], gs[s]) for s in group]
+            for s in group:
                 for j in range(NBR):
-                    before = meta[slots + slot + j]
+                    before = before_s[s, j, v]
                     cut = slice(j * HEAD, (j + 1) * HEAD)
-                    sum_k[slot + j + 1] = sum_k[before] + grad_k[cut]
-                    sum_v[slot + j + 1] = sum_v[before] + grad_v[cut]
+                    sum_k[slot[s] + j + 1] = sum_k[before] + grad_k[s][cut]
+                    sum_v[slot[s] + j + 1] = sum_v[before] + grad_v[s][cut]
             for when, event in events:
                 pl.when(v == min(when, spans - 1))(event)
             return carry
@@ -308,7 +364,7 @@
         lax.fori_loop(0, spans, step, 0)
 
         def gather(b, carry):
-            last = meta[2 * slots + b]
+            last = last_s[b // HEAD, b % HEAD]
             part[h][0, b] = sum_k[last].astype(BF16)
             part[h][1, b] = sum_v[last].astype(BF16)
             return carry
@@ -316,42 +372,45 @@
         lax.fori_loop(0, nz * PLANE, gather, 0)
 
     send_kv(0)
+    send_links()
+    wait_kv(0)
+    for turn in range(2):
+        ag_start(0, 1, turn)
     send_kv(1)
     send_qg(0)
-    wait_kv(0)
-    for kind in range(2):
-        ag_start(0, 1, kind)
-    send_qg(1)
-    for step in range(2, far + 1):
-        for kind in range(2):
-            ag_forward(0, step, kind)
+    chain_links()
+    forwards = [(step, turn) for step in range(2, far + 1) for turn in range(2)]
+    for i, (step, turn) in enumerate(forwards):
+        ag_forward(0, step, turn)
+        if i == 1:
+            send_qg(1)
     wait_kv(1)
-    for kind in range(2):
-        ag_start(1, 1, kind)
+    for turn in range(2):
+        ag_start(1, 1, turn)
     ag_last(0)
     wait_qg(0)
-    events = []
-    at = [4, 7, 11, 14, 16, 16]
-    for step in range(2, far + 1):
-        for kind in range(2):
-            events.append((at[len(events)], functools.partial(ag_forward, 1, step, kind)))
-    compute(0, events)
-    rs_send_step(0, 1)
-    send_out(0)
+    at = (AT_A0, AT_A1)
+    compute(0, [(at[i], functools.partial(ag_forward, 1, *forwards[i])) for i in range(min(2, len(forwards)))])
+    for i, (step, turn) in enumerate(forwards[2:]):
+        ag_forward(1, step, turn)
+        if i == 1:
+            send_out(0)
+    rs_begin(0)
     ag_last(1)
     wait_qg(1)
-    events = []
-    at = [3, 8, 14]
-    for step in range(2, far + 1):
-        events.append((at[len(events)], functools.partial(rs_step, 0, step)))
-    compute(1, events)
-    rs_send_step(1, 1)
+    sums = [(step, turn) for step in range(2, far + 1) for turn in range(2)]
+    at = (AT_B0, AT_B1, AT_B2)
+    compute(1, [(at[i], functools.partial(rs_step, 0, *sums[i])) for i in range(min(3, len(sums)))])
+    rs_begin(1)
+    for step, turn in sums[3:]:
+        rs_step(0, step, turn)
     send_out(1)
     rs_last(0)
-    for step in range(2, far + 1):
-        rs_step(1, step)
+    for step, turn in sums:
+        rs_step(1, step, turn)
     rs_last(1)
 
+    wait_bytes(links.at[pl.ds(0, nx - 1)], link_send)
     wait_in_sends()
     for h in range(2):
         for way in range(2):
@@ -359,8 +418,8 @@
                 for kind in range(2):
                     if ag_has(way, step, kind):
                         ag_copy(h, way, step, kind).wait_send()
-                ref = half[h].at[way] if step == 1 else full[h].at[way, step - 2]
-                wait_bytes(ref, rs_send.at[h, way, step - 1])
+                    if rs_has(way, step, kind):
+                        wait_bytes(rs_dst(h, way, step, kind), rs_send.at[h, way, step - 1, kind])
         wait_bytes(dkv_out.at[:, 0, :, pl.ds(0, (np_ - 1) * HEAD)], out_send.at[h])
         for k, dst in enumerate((ctx_out, dq_out)):
             wait_bytes(dst.at[0, :, pl.ds(0, (np_ - 1) * HEAD)], out_send.at[2 + 2 * k + h])
@@ -368,21 +427,12 @@
         wait_bytes(dst, out_recv.at[k])
 
 
-def make_meta(neighbours, nz, nx):
-    nblk = nz * PLANE
+def plane_links(neighbours, nz):
     z = lax.axis_index("seq") // PLANE
-    links = lax.all_gather(neighbours[0], "grp", axis=0, tiled=False)
-    per_plane = links.shape[1] // nz
-    links = jnp.concatenate([jnp.zeros((nx, 1, NBR), jnp.int32), links], 1)
+    per_plane = neighbours.shape[1] // nz
+    links = jnp.pad(neighbours[0].T, ((0, 8 - NBR), (1, 0)))
     links = lax.dynamic_slice_in_dim(links, z * per_plane, per_plane + 1, 1)
-    links = jnp.transpose(links, (1, 0, 2)).reshape(-1)
-    n = links.shape[0]
-    ids = jnp.arange(n, dtype=jnp.int32)
-    same = (links[:, None] == links[None, :]) & (ids[None, :] < ids[:, None])
-    before = jnp.max(jnp.where(same, ids[None, :] + 1, 0), axis=1)
-    here = links[None, :] == jnp.arange(nblk, dtype=jnp.int32)[:, None]
-    last = jnp.max(jnp.where(here, ids[None, :] + 1, 0), axis=1)
-    return jnp.concatenate([links, before, last])
+    return jnp.pad(links, ((0, 0), (0, HEAD - per_plane - 1)))
 
 
 def solution(mesh):
@@ -391,7 +441,7 @@
     far = nz // 2
 
     def step(queries, keys_values, neighbours, grad_context):
-        meta = make_meta(neighbours, nz, nx)
+        links = plane_links(neighbours, nz)
         tokens = queries.shape[1]
         nblk = nz * PLANE
         long_in = 16 + PLANE * tokens + SPAN
@@ -409,8 +459,10 @@
             + twice((2, max(far - 1, 1), 2, PLANE, HEAD, HEAD))
             + twice((2, PLANE, HEAD, HEAD))
             + [pltpu.VMEM((nx, SPAN, HEAD), F32)] * 2
-            + [sem((6,)), sem((6,)), sem((2, 2, far, 2)), sem((2, 2, far, 2)),
-               sem((2, 2, far)), sem((2, 2, far)), sem((6,)), sem((3,))]
+            + [pltpu.VMEM((nx, 8, HEAD), jnp.int32)] * 2 + [pltpu.VMEM((8, HEAD), jnp.int32)]
+            + [pltpu.SMEM((nx, 8, HEAD), jnp.int32)] * 2 + [pltpu.SMEM((8, HEAD), jnp.int32)]
+            + [sem, sem((3,)), sem((6,)), sem((6,))] + [sem((2, 2, far, 2))] * 4
+            + [sem((6,)), sem((3,))]
         )
         hbm = pl.BlockSpec(memory_space=pl.ANY)
         out = pl.pallas_call(
@@ -420,14 +472,14 @@
                 jax.ShapeDtypeStruct(queries.shape, BF16),
                 jax.ShapeDtypeStruct(keys_values.shape, BF16),
             ),
-            in_specs=[pl.BlockSpec(memory_space=pltpu.SMEM), hbm, hbm, hbm],
+            in_specs=[hbm, hbm, hbm, hbm],
             out_specs=(hbm, hbm, hbm),
             scratch_shapes=scratch,
             compiler_params=pltpu.CompilerParams(
                 collective_id=0, has_side_effects=True, vmem_limit_bytes=60 * 1024 * 1024
             ),
             name="plane_attention",
-        )(meta, queries, keys_values, grad_context)
+        )(links, queries, keys_values, grad_context)
         return tuple(out)
 
     in_specs = (

time: 235 us -> 212 us (0.902)
  Pallas kernels: 218 us -> 204 us
  blocking collectives: 8.78 us -> 0 us
    pallas_call x1, Pallas kernels: 218 us -> 204 us  [step(): pl.pallas_call(functools.partial(kernel, nz, nx), out_shape=(jax.ShapeDty...]
    all_gather x1 -> x0, blocking collectives: 8.78 us -> none  [make_meta(): links = lax.all_gather(neighbours[0], 'grp', axis=0, tiled=False)]
where the time goes in v2:
time: 212 us
  Pallas kernels  204 us (96%)
  local copies, waits for them, and re-layouts  7.53 us (4%)
    pallas_call x1, Pallas kernels, step(): pl.pallas_call(functools.partial(kernel, nz, nx), out_shape=(jax.ShapeDty...  204 us
    unnamed x7, local copies, waits for them, and re-layouts  6.18 us

profile of v2, /device:TPU:1, one launch (start us, length us, event | category | flops | bytes accessed | tf_op | source)
XLA Modules:
  0.0 212.1 jit_solution(7037171967044069629)
XLA Ops:
  0.6 0.8 pad_dynamic-slice_fusion
  1.4 0.6 pad.9.links_in
  2.0 203.9 %plane_attention.1 = (bf16[1,128,8192]{2,1,0:T(8,128)(2,1)}, bf16[1,128,8192]{2,1,0:T(8,128)(2,1)}, bf16[2,1,32,8192]{3,2,1,0:T(8,128)(2,1)}) custom-call(s32[8,128]{1,0:T(8,128)} %pad.9.links_in, bf16[1,128,8192]{2,1,0:T(8,128)(2,1)} %q_in.1, bf16[2,1,32,8192]{3,2,1,0:T(8,128)(2,1)} %kv_in.1, bf16[1,128,8192]{2,1,0:T(8,128)(2,1)} %g_in.1), custom_call_target="tpu_custom_call" | custom-call | tf_op jit(solution)/shard_map/plane_attention/pallas_call | solution.py:468
  205.9 0.0 copy-start
  205.9 3.2 %copy.10 = bf16[1,128,8192]{2,1,0:T(8,128)(2,1)} copy(bf16[1,128,8192]{2,1,0:T(8,128)(2,1)} %get-tuple-element.6) | data formatting | bytes 4194304
  209.1 0.0 copy-done
  209.1 0.0 copy-start.1
  209.1 1.3 copy.11
  210.5 0.6 copy-done.1
  211.1 1.0 copy.12
Async XLA Ops:
  205.9 3.3 %copy-start = (bf16[1,128,8192]{2,1,0:T(8,128)(2,1)S(1)}, bf16[1,128,8192]{2,1,0:T(8,128)(2,1)}, u32[]{:S(2)}) copy-start(bf16[1,128,8192]{2,1,0:T(8,128)(2,1)} %get-tuple-element.7) | copy-start | bytes 6291460
  209.1 2.0 copy-start.1

commit v3 on v2

--- a/solution.py
+++ b/solution.py
@@ -11,8 +11,8 @@
 SPAN = 64
 NBR = 2
 HEAD = 128
-AT_A0, AT_A1 = 6, 12
-AT_B0, AT_B1, AT_B2 = 4, 9, 14
+AT_A = (5, 11)
+AT_B = (2, 5, 10, 15)
 PLANE = 8
 MESH = pl.DeviceIdType.MESH
 BF16 = jnp.bfloat16
@@ -99,21 +99,22 @@
     def blk_rows(k):
         return pl.ds(pl.multiple_of(k * rows, rows), rows)
 
-    def kv_dst(h):
-        return kv[h].at[:, seq, blk_rows(x), :]
+    def kv_dst(h, kinds):
+        return kv[h].at[kinds, seq, blk_rows(x), :]
 
     def q_dst(buf):
         return buf.at[x, tok_rows(yc), :]
 
-    def send_kv(h):
+    def send_kv(h, kinds, sem):
         def body(r, carry):
             m, px, pyc = peer(r)
             pltpu.make_async_remote_copy(
-                src_ref=kv_in.at[:, 0, :, columns(m, h)], dst_ref=kv_dst(h),
-                send_sem=in_send.at[h], recv_sem=in_recv.at[h],
+                src_ref=kv_in.at[kinds, 0, :, columns(m, h)], dst_ref=kv_dst(h, kinds),
+                send_sem=in_send.at[h], recv_sem=in_recv.at[sem],
                 device_id=(z * PLANE + pyc, px), device_id_type=MESH).start()
             return carry
-        pltpu.make_async_copy(kv_in.at[:, 0, :, columns(me, h)], kv_dst(h), in_recv.at[h]).start()
+        pltpu.make_async_copy(
+            kv_in.at[kinds, 0, :, columns(me, h)], kv_dst(h, kinds), in_recv.at[sem]).start()
         lax.fori_loop(1, np_, body, 0)
 
     def send_qg(h):
@@ -134,8 +135,8 @@
     def wait_bytes(ref, sem):
         pltpu.make_async_copy(ref, ref, sem).wait()
 
-    def wait_kv(h):
-        wait_bytes(kv[h].at[:, zone(z)], in_recv.at[h])
+    def wait_kv(h, kinds, sem):
+        wait_bytes(kv[h].at[kinds, zone(z)], in_recv.at[sem])
 
     def wait_qg(h):
         for k, buf in enumerate((q[h], g[h])):
@@ -192,53 +193,45 @@
         for copy in copies:
             copy.wait()
 
+    def zone_part(zz, way, split):
+        if split:
+            return pl.ds(zz * PLANE + way * (PLANE // 2), PLANE // 2)
+        return zone(zz)
+
+    def ag_ref(h, way, step, kind, hops):
+        return kv[h].at[kind, zone_part(near((2 * way - 1) * hops), way, step == far)]
+
     def ag_copy(h, way, step, kind):
-        sign = 1 - 2 * way
-        part_ref = kv[h].at[kind, zone(near(-sign * (step - 1)))]
+        ref = ag_ref(h, way, step, kind, step - 1)
         return pltpu.make_async_remote_copy(
-            src_ref=part_ref, dst_ref=part_ref,
+            src_ref=ref, dst_ref=ref,
             send_sem=ag_send.at[h, way, step - 1, kind], recv_sem=ag_recv.at[h, way, step - 1, kind],
-            device_id=z_device(sign), device_id_type=MESH)
-
-    def ag_has(way, step, kind):
-        return step < far or kind == way
-
-    def ag_start(h, step, turn):
+            device_id=z_device(1 - 2 * way), device_id_type=MESH)
+
+    def ag_start(h, kind):
         for way in range(2):
-            kind = way if turn == 0 else 1 - way
-            if ag_has(way, step, kind):
-                ag_copy(h, way, step, kind).start()
+            ag_copy(h, way, 1, kind).start()
 
     def ag_wait(h, way, step, kind):
-        sign = 1 - 2 * way
-        wait_bytes(kv[h].at[kind, zone(near(-sign * step))], ag_recv.at[h, way, step - 1, kind])
-
-    def ag_forward(h, step, turn):
+        wait_bytes(ag_ref(h, way, step, kind, step), ag_recv.at[h, way, step - 1, kind])
+
+    def ag_forward(h, step, kind):
         for way in range(2):
-            kind = way if turn == 0 else 1 - way
             ag_wait(h, way, step - 1, kind)
-            if ag_has(way, step, kind):
-                ag_copy(h, way, step, kind).start()
+            ag_copy(h, way, step, kind).start()
 
     def ag_last(h):
         for kind in range(2):
             for way in range(2):
-                if ag_has(way, far, kind):
-                    ag_wait(h, way, far, kind)
-
-    def rs_has(way, step, kind):
-        return step > 1 or kind == way
+                ag_wait(h, way, far, kind)
 
     def rs_dst(h, way, step, kind):
-        return half[h].at[way] if step == 1 else full[h].at[way, step - 2, kind]
-
-    def rs_base(way, step):
-        return near((1 - 2 * way) * (far + 1 - step)) * PLANE
+        return half[h].at[way, kind] if step == 1 else full[h].at[way, step - 2, kind]
 
     def rs_send_part(h, way, step, kind):
+        zz = near((1 - 2 * way) * (far + 1 - step))
         pltpu.make_async_remote_copy(
-            src_ref=part[h].at[kind, pl.ds(pl.multiple_of(rs_base(way, step), PLANE), PLANE)],
-            dst_ref=rs_dst(h, way, step, kind),
+            src_ref=part[h].at[kind, zone_part(zz, way, step == 1)], dst_ref=rs_dst(h, way, step, kind),
             send_sem=rs_send.at[h, way, step - 1, kind], recv_sem=rs_recv.at[h, way, step - 1, kind],
             device_id=z_device(1 - 2 * way), device_id_type=MESH).start()
 
@@ -246,54 +239,51 @@
         wait_bytes(rs_dst(h, way, step, kind), rs_recv.at[h, way, step - 1, kind])
 
     def rs_begin(h):
+        for kind in range(2):
+            for way in range(2):
+                rs_send_part(h, way, 1, kind)
+
+    def rs_step(h, step, kind):
         for way in range(2):
-            rs_send_part(h, way, 1, way)
-        for way in range(2):
-            if far > 1:
-                rs_send_part(h, way, 2, 1 - way)
-
-    def rs_step(h, step, turn):
-        for way in range(2):
-            kind = way if turn == 0 else 1 - way
-            if not rs_has(way, step - 1, kind):
-                continue
-            base = rs_base(way, step)
             rs_wait(h, way, step - 1, kind)
             got = rs_dst(h, way, step - 1, kind)
+            base = near((1 - 2 * way) * (far + 1 - step)) * PLANE
+            if step == 2:
+                base = base + way * (PLANE // 2)
 
             def add(b, carry):
                 part[h][kind, base + b] = (
                     part[h][kind, base + b].astype(F32) + got[b].astype(F32)).astype(BF16)
                 return carry
 
-            lax.fori_loop(0, PLANE, add, 0)
+            lax.fori_loop(0, PLANE // 2 if step == 2 else PLANE, add, 0)
             rs_send_part(h, way, step, kind)
 
-    def rs_last(h):
-        for kind in range(2):
-            ways = [way for way in range(2) if rs_has(way, far, kind)]
-            for way in ways:
-                rs_wait(h, way, far, kind)
-
-            def add(b, carry):
-                total = part[h][kind, z * PLANE + b].astype(F32)
-                for way in ways:
-                    total += rs_dst(h, way, far, kind)[b].astype(F32)
-                own[h][kind, b] = total.astype(BF16)
-                return carry
-
-            lax.fori_loop(0, PLANE, add, 0)
-
+    def rs_last(h, kind):
+        for way in range(2):
+            rs_wait(h, way, far, kind)
+
+        def add(b, carry):
+            total = part[h][kind, z * PLANE + b].astype(F32)
+            for way in range(2):
+                total += rs_dst(h, way, far, kind)[b].astype(F32)
+            own[h][kind, b] = total.astype(BF16)
+            return carry
+
+        lax.fori_loop(0, PLANE, add, 0)
+
+    def send_own(h, kinds):
         def body(r, carry):
             m, px, pyc = peer(r)
             pltpu.make_async_remote_copy(
-                src_ref=own[h].at[:, pyc, blk_rows(px), :], dst_ref=dkv_out.at[:, 0, :, columns(me, h)],
+                src_ref=own[h].at[kinds, pyc, blk_rows(px), :], dst_ref=dkv_out.at[kinds, 0, :, columns(me, h)],
                 send_sem=out_send.at[h], recv_sem=out_recv.at[0],
                 device_id=(z * PLANE + pyc, px), device_id_type=MESH).start()
             return carry
 
         pltpu.make_async_copy(
-            own[h].at[:, yc, blk_rows(x), :], dkv_out.at[:, 0, :, columns(me, h)], out_recv.at[0]).start()
+            own[h].at[kinds, yc, blk_rows(x), :], dkv_out.at[kinds, 0, :, columns(me, h)],
+            out_recv.at[0]).start()
         lax.fori_loop(1, np_, body, 0)
 
     def out_rows(k):
@@ -371,44 +361,48 @@
 
         lax.fori_loop(0, nz * PLANE, gather, 0)
 
-    send_kv(0)
+    both = pl.ds(0, 2)
+    for kind in range(2):
+        send_kv(0, pl.ds(kind, 1), 6 * kind)
     send_links()
-    wait_kv(0)
-    for turn in range(2):
-        ag_start(0, 1, turn)
-    send_kv(1)
+    for kind in range(2):
+        wait_kv(0, pl.ds(kind, 1), 6 * kind)
+        ag_start(0, kind)
+    send_kv(1, both, 1)
     send_qg(0)
     chain_links()
-    forwards = [(step, turn) for step in range(2, far + 1) for turn in range(2)]
-    for i, (step, turn) in enumerate(forwards):
-        ag_forward(0, step, turn)
+    steps = [(step, kind) for step in range(2, far + 1) for kind in range(2)]
+    for i, (step, kind) in enumerate(steps):
+        ag_forward(0, step, kind)
         if i == 1:
             send_qg(1)
-    wait_kv(1)
-    for turn in range(2):
-        ag_start(1, 1, turn)
+    wait_kv(1, both, 1)
+    for kind in range(2):
+        ag_start(1, kind)
     ag_last(0)
     wait_qg(0)
-    at = (AT_A0, AT_A1)
-    compute(0, [(at[i], functools.partial(ag_forward, 1, *forwards[i])) for i in range(min(2, len(forwards)))])
-    for i, (step, turn) in enumerate(forwards[2:]):
-        ag_forward(1, step, turn)
+    compute(0, [(when, functools.partial(ag_forward, 1, *todo)) for when, todo in zip(AT_A, steps)])
+    for i, (step, kind) in enumerate(steps[len(AT_A):]):
+        ag_forward(1, step, kind)
         if i == 1:
             send_out(0)
     rs_begin(0)
     ag_last(1)
     wait_qg(1)
-    sums = [(step, turn) for step in range(2, far + 1) for turn in range(2)]
-    at = (AT_B0, AT_B1, AT_B2)
-    compute(1, [(at[i], functools.partial(rs_step, 0, *sums[i])) for i in range(min(3, len(sums)))])
+    compute(1, [(when, functools.partial(rs_step, 0, *todo)) for when, todo in zip(AT_B, steps)])
     rs_begin(1)
-    for step, turn in sums[3:]:
-        rs_step(0, step, turn)
-    send_out(1)
-    rs_last(0)
-    for step, turn in sums:
-        rs_step(1, step, turn)
-    rs_last(1)
+    for i, (step, kind) in enumerate(steps[len(AT_B):]):
+        rs_step(0, step, kind)
+        if i == 1:
+            send_out(1)
+    for kind in range(2):
+        rs_last(0, kind)
+    send_own(0, both)
+    for step, kind in steps:
+        rs_step(1, step, kind)
+    for kind in range(2):
+        rs_last(1, kind)
+        send_own(1, pl.ds(kind, 1))
 
     wait_bytes(links.at[pl.ds(0, nx - 1)], link_send)
     wait_in_sends()
@@ -416,15 +410,39 @@
         for way in range(2):
             for step in range(1, far + 1):
                 for kind in range(2):
-                    if ag_has(way, step, kind):
-                        ag_copy(h, way, step, kind).wait_send()
-                    if rs_has(way, step, kind):
-                        wait_bytes(rs_dst(h, way, step, kind), rs_send.at[h, way, step - 1, kind])
+                    ag_copy(h, way, step, kind).wait_send()
+                    wait_bytes(rs_dst(h, way, step, kind), rs_send.at[h, way, step - 1, kind])
         wait_bytes(dkv_out.at[:, 0, :, pl.ds(0, (np_ - 1) * HEAD)], out_send.at[h])
         for k, dst in enumerate((ctx_out, dq_out)):
             wait_bytes(dst.at[0, :, pl.ds(0, (np_ - 1) * HEAD)], out_send.at[2 + 2 * k + h])
     for k, dst in enumerate((dkv_out, ctx_out, dq_out)):
         wait_bytes(dst, out_recv.at[k])
+
+
+def finish(a, b, c):
+    def body(*refs):
+        sems = refs[6]
+        copies = []
+        for k in range(3):
+            rows = refs[k].shape[-2] // 2
+            lead = (slice(None),) * (len(refs[k].shape) - 2)
+            for part in range(2):
+                at = lead + (pl.ds(part * rows, rows),)
+                copies.append(pltpu.make_async_copy(
+                    refs[k].at[at], refs[3 + k].at[at], sems.at[2 * k + part]))
+        for copy in copies:
+            copy.start()
+        for copy in copies:
+            copy.wait()
+
+    hbm = pl.BlockSpec(memory_space=pl.ANY)
+    return pl.pallas_call(
+        body,
+        out_shape=tuple(jax.ShapeDtypeStruct(t.shape, t.dtype) for t in (a, b, c)),
+        in_specs=[hbm] * 3, out_specs=(hbm,) * 3,
+        scratch_shapes=[pltpu.SemaphoreType.DMA((6,))],
+        name="results",
+    )(a, b, c)
 
 
 def plane_links(neighbours, nz):
@@ -455,13 +473,13 @@
             + twice((nx, long_out, HEAD)) + twice((nx, long_out, HEAD))
             + [pltpu.VMEM((slots + 1, HEAD, HEAD), F32)] * 2
             + twice((2, nblk, HEAD, HEAD))
-            + twice((2, PLANE, HEAD, HEAD))
+            + twice((2, 2, PLANE // 2, HEAD, HEAD))
             + twice((2, max(far - 1, 1), 2, PLANE, HEAD, HEAD))
             + twice((2, PLANE, HEAD, HEAD))
             + [pltpu.VMEM((nx, SPAN, HEAD), F32)] * 2
             + [pltpu.VMEM((nx, 8, HEAD), jnp.int32)] * 2 + [pltpu.VMEM((8, HEAD), jnp.int32)]
             + [pltpu.SMEM((nx, 8, HEAD), jnp.int32)] * 2 + [pltpu.SMEM((8, HEAD), jnp.int32)]
-            + [sem, sem((3,)), sem((6,)), sem((6,))] + [sem((2, 2, far, 2))] * 4
+            + [sem, sem((3,)), sem((6,)), sem((7,))] + [sem((2, 2, far, 2))] * 4
             + [sem((6,)), sem((3,))]
         )
         hbm = pl.BlockSpec(memory_space=pl.ANY)

time: 212 us -> 205 us (0.967)
  Pallas kernels: 204 us -> 197 us
    pallas_call x1, Pallas kernels: 204 us -> 197 us  [step(): pl.pallas_call(functools.partial(kernel, nz, nx), out_shape=(jax.ShapeDty...]
where the time goes in v3:
time: 205 us
  Pallas kernels  197 us (96%)
  local copies, waits for them, and re-layouts  7.53 us (4%)
    pallas_call x1, Pallas kernels, step(): pl.pallas_call(functools.partial(kernel, nz, nx), out_shape=(jax.ShapeDty...  197 us
    unnamed x7, local copies, waits for them, and re-layouts  6.18 us

profile of v3, /device:TPU:1, one launch (start us, length us, event | category | flops | bytes accessed | tf_op | source)
XLA Modules:
  0.0 205.3 jit_solution(6025219788209276344)
XLA Ops:
  0.6 0.8 pad_dynamic-slice_fusion
  1.4 0.6 pad.9.links_in
  2.0 197.1 %plane_attention.1 = (bf16[1,128,8192]{2,1,0:T(8,128)(2,1)}, bf16[1,128,8192]{2,1,0:T(8,128)(2,1)}, bf16[2,1,32,8192]{3,2,1,0:T(8,128)(2,1)}) custom-call(s32[8,128]{1,0:T(8,128)} %pad.9.links_in, bf16[1,128,8192]{2,1,0:T(8,128)(2,1)} %q_in.1, bf16[2,1,32,8192]{3,2,1,0:T(8,128)(2,1)} %kv_in.1, bf16[1,128,8192]{2,1,0:T(8,128)(2,1)} %g_in.1), custom_call_target="tpu_custom_call" | custom-call | tf_op jit(solution)/shard_map/plane_attention/pallas_call | solution.py:486
  199.1 0.0 copy-start
  199.1 3.2 %copy.10 = bf16[1,128,8192]{2,1,0:T(8,128)(2,1)} copy(bf16[1,128,8192]{2,1,0:T(8,128)(2,1)} %get-tuple-element.6) | data formatting | bytes 4194304
  202.4 0.0 copy-done
  202.4 0.0 copy-start.1
  202.4 1.3 copy.11
  203.7 0.6 copy-done.1
  204.3 1.0 copy.12
Async XLA Ops:
  199.1 3.3 %copy-start = (bf16[1,128,8192]{2,1,0:T(8,128)(2,1)S(1)}, bf16[1,128,8192]{2,1,0:T(8,128)(2,1)}, u32[]{:S(2)}) copy-start(bf16[1,128,8192]{2,1,0:T(8,128)(2,1)} %get-tuple-element.7) | copy-start | bytes 6291460
  202.4 2.0 copy-start.1

commit v4 on v3

--- a/solution.py
+++ b/solution.py
@@ -419,30 +419,40 @@
         wait_bytes(dst, out_recv.at[k])
 
 
-def finish(a, b, c):
+def results(*arrays):
+    n = len(arrays)
+
     def body(*refs):
-        sems = refs[6]
-        copies = []
-        for k in range(3):
-            rows = refs[k].shape[-2] // 2
-            lead = (slice(None),) * (len(refs[k].shape) - 2)
-            for part in range(2):
-                at = lead + (pl.ds(part * rows, rows),)
-                copies.append(pltpu.make_async_copy(
-                    refs[k].at[at], refs[3 + k].at[at], sems.at[2 * k + part]))
-        for copy in copies:
+        src, dst, held, (sem_in, sem_out) = refs[:n], refs[n:2 * n], refs[2 * n:3 * n], refs[3 * n:]
+        cuts = []
+        for k in range(n):
+            rows = src[k].shape[-2]
+            for lead in range(src[k].shape[0]):
+                for r in range(0, rows, 32):
+                    cuts.append((k, (lead,) + (0,) * (len(src[k].shape) - 3) + (pl.ds(r, 32),)))
+        loads = [pltpu.make_async_copy(src[k].at[at], held[k].at[at], sem_in.at[i])
+                 for i, (k, at) in enumerate(cuts)]
+        stores = [pltpu.make_async_copy(held[k].at[at], dst[k].at[at], sem_out.at[i])
+                  for i, (k, at) in enumerate(cuts)]
+        for copy in loads:
             copy.start()
-        for copy in copies:
+        for load, store in zip(loads, stores):
+            load.wait()
+            store.start()
+        for copy in stores:
             copy.wait()
 
     hbm = pl.BlockSpec(memory_space=pl.ANY)
+    count = sum(t.shape[0] * (t.shape[-2] // 32) for t in arrays)
     return pl.pallas_call(
         body,
-        out_shape=tuple(jax.ShapeDtypeStruct(t.shape, t.dtype) for t in (a, b, c)),
-        in_specs=[hbm] * 3, out_specs=(hbm,) * 3,
-        scratch_shapes=[pltpu.SemaphoreType.DMA((6,))],
+        out_shape=tuple(jax.ShapeDtypeStruct(t.shape, t.dtype) for t in arrays),
+        in_specs=[hbm] * n, out_specs=(hbm,) * n,
+        scratch_shapes=[pltpu.VMEM(t.shape, t.dtype) for t in arrays]
+        + [pltpu.SemaphoreType.DMA((count,))] * 2,
+        compiler_params=pltpu.CompilerParams(vmem_limit_bytes=60 * 1024 * 1024),
         name="results",
-    )(a, b, c)
+    )(*arrays)
 
 
 def plane_links(neighbours, nz):
@@ -498,7 +508,7 @@
             ),
             name="plane_attention",
         )(links, queries, keys_values, grad_context)
-        return tuple(out)
+        return tuple(results(*out))
 
     in_specs = (
         P("grp", "seq", None),

time: 205 us -> 204 us (level)
  local copies, waits for them, and re-layouts: 7.53 us -> 1.36 us
  Pallas kernels: 197 us -> 202 us
    unnamed x7 -> x0, local copies, waits for them, and re-layouts: 6.18 us -> none
    pallas_call x0 -> x1, Pallas kernels: none -> 4.71 us  [results(): pl.pallas_call(body, out_shape=tuple((jax.ShapeDtypeStruct(t.shape, t.dty...]
where the time goes in v4:
time: 204 us
  Pallas kernels  202 us (99%)
    pallas_call x1, Pallas kernels, step(): pl.pallas_call(functools.partial(kernel, nz, nx), out_shape=(jax.ShapeDty...  197 us
    pallas_call x1, Pallas kernels, results(): pl.pallas_call(body, out_shape=tuple((jax.ShapeDtypeStruct(t.shape, t.dty...  4.71 us

profile of v4, /device:TPU:1, one launch (start us, length us, event | category | flops | bytes accessed | tf_op | source)
XLA Modules:
  0.0 204.0 jit_solution(6275438669633496178)
XLA Ops:
  0.6 0.8 pad_dynamic-slice_fusion
  1.4 0.6 pad.9.links_in
  2.0 197.3 %plane_attention.1 = (bf16[1,128,8192]{2,1,0:T(8,128)(2,1)}, bf16[1,128,8192]{2,1,0:T(8,128)(2,1)}, bf16[2,1,32,8192]{3,2,1,0:T(8,128)(2,1)}) custom-call(s32[8,128]{1,0:T(8,128)} %pad.9.links_in, bf16[1,128,8192]{2,1,0:T(8,128)(2,1)} %q_in.1, bf16[2,1,32,8192]{3,2,1,0:T(8,128)(2,1)} %kv_in.1, bf16[1,128,8192]{2,1,0:T(8,128)(2,1)} %g_in.1), custom_call_target="tpu_custom_call" | custom-call | tf_op jit(solution)/shard_map/plane_attention/pallas_call | solution.py:496
  199.3 4.7 %results.1 = (bf16[1,128,8192]{2,1,0:T(8,128)(2,1)}, bf16[1,128,8192]{2,1,0:T(8,128)(2,1)}, bf16[2,1,32,8192]{3,2,1,0:T(8,128)(2,1)}) custom-call(bf16[1,128,8192]{2,1,0:T(8,128)(2,1)} %get-tuple-element.6.refs_0_, bf16[1,128,8192]{2,1,0:T(8,128)(2,1)} %get-tuple-element.7.refs_1_, bf16[2,1,32,8192]{3,2,1,0:T(8,128)(2,1)} %get-tuple-element.8.refs_2_), custom_call_target="tpu_custom_call" | custom-call | tf_op jit(solution)/shard_map/results/pallas_call | solution.py:447
